TPU v7x, 32 devices: a whole 2x2x4 slice. The times are simulated.
32 devices in a mesh: tm: 4 (over z), space: 8 (over y, x, core).
Axes of the slice: x: 2, y: 2, z: 4, core: 2. Of those that a mesh axis runs over, the one named last changes fastest.
Arguments:
- frames: bfloat16 [4, 73, 64, 1024], P('tm', None, None, 'space'), may hold values from -6 to 6
- regrid_mats: bfloat16 [16, 64, 144], replicated, may hold values from -0.75 to 0.75
- pair_source: int32 [1024], P('space'), may hold values from 0 to 127
- pair_matrix: int32 [1024], P('space'), may hold values from 0 to 15
- pair_device: int32 [1024, 1], P('space'), may hold values from 0 to 7; in each aligned block of 128 rows (0 to 127, 128 to 255, ...) at most 24 rows name the same one
- pair_local: int32 [1024], P('space'), may hold values from 0 to 11
- w_first: bfloat16 [3, 3, 73, 256], replicated, may hold values from -0.25 to 0.25
- b_first: float32 [256], replicated, may hold values from -3 to 3
- w_second: bfloat16 [3, 3, 256, 256], replicated, may hold values from -0.125 to 0.125
- b_second: float32 [256], replicated, may hold values from -3 to 3
Outputs:
- features: bfloat16 [4, 96, 64, 256], P('tm', 'space')
Inputs may be any that keep to these rules, and one draw needn't show every extreme that they name: `pair_device`: among the 128 rows of one device no device number appears more than 24 times, and in every draw some device's rows name one device exactly 24 times.
All inputs are finite; a program needn't handle non-finite values.
Results may differ from a plain program's by a relative error of at most 0.0064.
Values may be sent and summed in bfloat16 or wider, within the bound.
A program may use at most 64 MiB of HBM per device.

v0:
```python
import jax
import jax.numpy as jnp
from jax import lax
from jax.sharding import PartitionSpec as P

SIDE = 8
SB = 64
BLK_DEV = 12
PAD_SIDE = 12


def conv_valid(inputs, weights, layout):
    return lax.conv_general_dilated(
        inputs,
        weights,
        (1, 1),
        "VALID",
        dimension_numbers=layout,
        preferred_element_type=jnp.float32,
    )


def per_device(
    frames,
    regrid_mats,
    pair_source,
    pair_matrix,
    pair_device,
    pair_local,
    w_first,
    b_first,
    w_second,
    b_second,
):
    devices = lax.axis_size("space")
    band_rows = lax.all_to_all(frames, "space", split_axis=2, concat_axis=3, tiled=True)
    local_times = band_rows.shape[0]
    variables = band_rows.shape[1]
    source = band_rows.reshape(local_times, variables, -1, SB)
    pair_count = pair_source.shape[0]
    capacity = max(2, 3 * pair_count // (2 * devices))
    flat_count = devices * capacity
    target = pair_device[:, 0]
    matches = (target[:, None] == jnp.arange(devices, dtype=jnp.int32)[None, :]).astype(jnp.int32)
    ranking = jnp.sum(matches * (jnp.cumsum(matches, axis=0) - 1), axis=1)
    places = target * capacity + ranking
    block_slots = (
        jnp.full((flat_count,), BLK_DEV, jnp.int32)
        .at[places]
        .set(pair_local)
        .reshape(devices, capacity)
    )
    picked = jnp.take(source, pair_source, axis=2)
    shipped = jnp.transpose(picked, (2, 0, 1, 3))
    outgoing = (
        jnp.zeros((flat_count, local_times, variables, SB), jnp.bfloat16).at[places].set(shipped)
    )
    outgoing = outgoing.reshape(devices, capacity, local_times, variables, SB)
    matrix_slots = (
        jnp.zeros((flat_count,), jnp.int32).at[places].set(pair_matrix).reshape(devices, capacity)
    )
    rows_part = lax.all_to_all(outgoing, "space", split_axis=0, concat_axis=0, tiled=True)
    matrix_part = lax.all_to_all(matrix_slots, "space", split_axis=0, concat_axis=0, tiled=True)
    block_part = lax.all_to_all(block_slots, "space", split_axis=0, concat_axis=0, tiled=True)
    matrices = jnp.take(regrid_mats, matrix_part, axis=0)
    partial_value = jnp.einsum(
        "nktvs,nksc->nktvc", rows_part, matrices, preferred_element_type=jnp.float32
    ).astype(jnp.bfloat16)
    selector = (
        block_part.reshape(1, flat_count) == jnp.arange(BLK_DEV, dtype=jnp.int32)[:, None]
    ).astype(jnp.bfloat16)
    summed = jnp.dot(
        selector, partial_value.reshape(flat_count, -1), preferred_element_type=jnp.float32
    )
    padded_field = summed.astype(jnp.bfloat16).reshape(
        BLK_DEV * local_times, variables, PAD_SIDE, PAD_SIDE
    )
    first_out = conv_valid(padded_field, w_first, ("NCHW", "HWIO", "NHWC")) + b_first
    hidden = jax.nn.gelu(first_out, approximate=True).astype(jnp.bfloat16)
    second = conv_valid(hidden, w_second, ("NHWC", "HWIO", "NHWC")) + b_second
    result = second.astype(jnp.bfloat16).reshape(BLK_DEV, local_times, SIDE * SIDE, -1)
    return jnp.transpose(result, (1, 0, 2, 3))


def solution(mesh):
    in_specs = (
        P("tm", None, None, "space"),
        P(),
        P("space"),
        P("space"),
        P("space", None),
        P("space"),
        P(),
        P(),
        P(),
        P(),
    )
    out_specs = P("tm", "space", None, None)
    return jax.shard_map(
        per_device, mesh=mesh, in_specs=in_specs, out_specs=out_specs, check_vma=False
    )
```

profile of v0, /device:TPU:0, one launch (start us, length us, event | category | flops | bytes accessed | tf_op | source)
XLA Modules:
  0.0 153.7 jit_solution(2055888904172793022)
XLA Ops:
  0.0 3.2 %copy.18 = bf16[1,73,64,128]{3,1,0,2:T(8,128)(2,1)} copy(bf16[1,73,64,128]{3,2,1,0:T(8,128)(2,1)} %param.10) | data formatting | bytes 2392064 | tf_op args[0]
  3.2 5.2 %all-to-all-start.1 = ((bf16[1,73,64,128]{3,1,0,2:T(8,128)(2,1)}), bf16[1,73,64,128]{3,1,0,2:T(8,128)(2,1)S(1)}, u32[]{:S(2)}, u32[]{:S(2)}) async-start(bf16[1,73,64,128]{3,1,0,2:T(8,128)(2,1)} %copy.18), calls=%async_computation.1 | async-start | bytes 2621440 | tf_op jit(solution)/shard_map/all_to_all | solution.py:36
  8.4 0.1 fusion.14
  8.5 0.2 reduce_window_sum.11
  8.7 0.2 select_reduce_fusion
  8.9 1.1 scatter_custom_fusion.2
  10.0 0.7 all_to_all.36
  10.7 15.9 %all-to-all-done.1 = bf16[1,73,64,128]{3,1,0,2:T(8,128)(2,1)S(1)} async-done(((bf16[1,73,64,128]{3,1,0,2:T(8,128)(2,1)}), bf16[1,73,64,128]{3,1,0,2:T(8,128)(2,1)S(1)}, u32[]{:S(2)}, u32[]{:S(2)}) %all-to-all-start.1) | async-done | bytes 1196064 | tf_op jit(solution)/shard_map/all_to_all | solution.py:36
  26.6 3.3 %all-to-all-start.3 = ((s32[8,1,24]{2,1,0:T(1,128)}), s32[8,1,24]{2,1,0:T(1,128)S(1)}, u32[]{:S(2)}, u32[]{:S(2)}) async-start(s32[8,1,24]{2,1,0:T(1,128)} %all_to_all.36), calls=%async_computation.3 | async-start | bytes 8192 | tf_op jit(solution)/shard_map/all_to_all | solution.py:63
  30.0 1.1 scatter_custom_fusion
  31.1 0.7 all_to_all.30
  31.7 2.6 %copy.25 = bf16[1,73,8,8,128]{1,4,3,2,0:T(8,128)(2,1)} copy(bf16[1,73,8,8,128]{4,1,2,3,0:T(8,128)(2,1)S(1)} %bitcast.41) | data formatting | bytes 2392064 | tf_op jit(solution)/shard_map/reshape | solution.py:39
  34.3 2.5 %gather_fusion = bf16[128,73,64]{1,2,0:T(8,128)(2,1)S(1)} fusion(bf16[73,128,64]{0,2,1:T(8,128)(2,1)} %bitcast.40, s32[1024]{0:T(1024)S(1)} %pad_clamp_fusion.1), kind=kCustom, calls=%fused_computation | custom fusion | bytes 2392576 | tf_op jit(solution)/shard_map/jit(_take)/gather | solution.py:53
  36.9 4.1 %all-to-all-start = ((s32[8,1,24]{2,1,0:T(1,128)}), s32[8,1,24]{2,1,0:T(1,128)S(1)}, u32[]{:S(2)}, u32[]{:S(2)}) async-start(s32[8,1,24]{2,1,0:T(1,128)} %all_to_all.30), calls=%async_computation | async-start | bytes 8192 | tf_op jit(solution)/shard_map/all_to_all | solution.py:64
  41.0 1.6 %fusion.4 = bf16[128,73,64]{1,2,0:T(8,128)(2,1)} fusion(bf16[128,73,64]{1,2,0:T(8,128)(2,1)S(1)} %gather_fusion, pred[128]{0:T(512)(128)(4,1)S(1)} %compare_and_fusion.1), kind=kLoop, calls=%fused_computation.13 | loop fusion | flops 598016 | bytes 2392192 | tf_op jit(solution)/shard_map/transpose | solution.py:54
  42.7 2.4 %broadcast.67 = bf16[192,73,64]{1,2,0:T(8,128)(2,1)} broadcast(bf16[]{:T(256)} %constant.28.clone.1), dimensions={} | broadcast | bytes 1794050 | tf_op jit(solution)/shard_map/broadcast_in_dim | solution.py:56
  45.1 15.7 %scatter_fusion = bf16[192,73,64]{1,2,0:T(8,128)(2,1)} fusion(bf16[192,73,64]{1,2,0:T(8,128)(2,1)} %broadcast.67, s32[128]{0:T(128)S(1)} %fusion.16, bf16[128,73,64]{1,2,0:T(8,128)(2,1)S(1)} %copy-done.2), kind=kCustom, calls=%fused_computation.3 | custom fusion | bytes 3588608 | tf_op jit(solution)/shard_map/scatter | solution.py:56
  60.8 4.8 %all-to-all-start.2 = ((bf16[8,24,1,73,64]{3,4,1,2,0:T(8,128)(2,1)}), bf16[8,24,1,73,64]{3,4,1,2,0:T(8,128)(2,1)}, u32[]{:S(2)}, u32[]{:S(2)}) async-start(bf16[8,24,1,73,64]{3,4,1,2,0:T(8,128)(2,1)} %bitcast.39), calls=%async_computation.2 | async-start | bytes 6291456 | tf_op jit(solution)/shard_map/all_to_all | solution.py:62
  65.6 0.1 reshape.97
  65.7 0.5 broadcast.88
  66.2 0.7 reduce.3
  66.8 0.1 eq.34
  66.9 8.1 %gather_fusion.1 = bf16[192,64,144]{2,1,0:T(8,128)(2,1)} fusion(bf16[16,64,144]{2,1,0:T(8,128)(2,1)S(1)} %copy-done.1, s32[1024]{0:T(1024)S(1)} %pad_clamp_fusion), kind=kCustom, calls=%fused_computation.1 | custom fusion | bytes 7078656 | tf_op jit(solution)/shard_map/jit(_take)/gather | solution.py:65
  75.0 28.5 %all-to-all-done.2 = bf16[8,24,1,73,64]{3,4,1,2,0:T(8,128)(2,1)} async-done(((bf16[8,24,1,73,64]{3,4,1,2,0:T(8,128)(2,1)}), bf16[8,24,1,73,64]{3,4,1,2,0:T(8,128)(2,1)}, u32[]{:S(2)}, u32[]{:S(2)}) %all-to-all-start.2) | async-done | bytes 1794080 | tf_op jit(solution)/shard_map/all_to_all | solution.py:62
  103.5 9.6 %convolution_convert_fusion.1 = bf16[8,24,73,144]{2,3,1,0:T(8,128)(2,1)} fusion(bf16[8,24,64,144]{3,2,1,0:T(8,128)(2,1)} %bitcast.38, pred[8,24]{1,0:T(8,128)(4,1)S(1)} %compare_and_fusion, bf16[8,24,1,73,64]{3,4,1,2,0:T(8,128)(2,1)} %all-to-all-done.2), kind=kOutput, calls=%fused_computation.6 | convolution fusion | flops 262130688 | bytes 9369792 | tf_op jit(solution)/shard_map/nktvs,nksc->nktvc/dot_general | solution.py:66
  113.1 10.9 %copy.22 = bf16[8,24,73,144]{3,2,1,0:T(8,128)(2,1)} copy(bf16[8,24,73,144]{2,3,1,0:T(8,128)(2,1)} %convolution_convert_fusion.1) | data formatting | bytes 8073216 | tf_op jit(solution)/shard_map/convert_element_type | solution.py:68
  124.0 12.1 %reshape.83 = bf16[192,10512]{1,0:T(8,128)(2,1)} reshape(bf16[8,24,73,144]{3,2,1,0:T(8,128)(2,1)} %copy.22) | data formatting | bytes 8073216 | tf_op jit(solution)/shard_map/reshape | solution.py:73
  136.1 2.8 %convolution_convert_fusion = bf16[12,10512]{1,0:T(8,128)(2,1)S(1)} fusion(bf16[192,10512]{1,0:T(8,128)(2,1)} %reshape.83, s32[192]{0:T(256)S(1)} %eq.34), kind=kOutput, calls=%fused_computation.5 | convolution fusion | flops 48567744 | bytes 4289664 | tf_op jit(solution)/shard_map/dot_general | solution.py:72
  138.9 4.5 %reshape.84 = bf16[12,73,12,12]{3,2,1,0:T(8,128)(2,1)} reshape(bf16[12,10512]{1,0:T(8,128)(2,1)S(1)} %convolution_convert_fusion) | data formatting | bytes 504576 | tf_op jit(solution)/shard_map/reshape | solution.py:75
  143.4 6.2 %copy.23 = bf16[12,73,12,12]{1,0,3,2:T(8,128)(2,1)S(1)} copy(bf16[12,73,12,12]{3,2,1,0:T(8,128)(2,1)} %reshape.84) | data formatting | bytes 504576 | tf_op jit(solution)/shard_map/reshape | solution.py:75
  149.6 3.3 %fusion.13 = bf16[12,8,8,256]{3,0,2,1:T(8,128)(2,1)S(1)} fusion(bf16[3,3,256,256]{3,2,1,0:T(8,128)(2,1)S(1)} %copy-done, bf16[12,73,12,12]{1,0,3,2:T(8,128)(2,1)S(1)} %copy.23, bf16[3,3,73,256]{3,2,1,0:T(8,128)(2,1)S(1)} %copy-done.4, f32[256]{0:T(256)S(1)} %copy-done.5, f32[256]{0:T(256)S(1)} %copy-done.6), kind=kOutput, calls=%fused_computation.23 | convolution fusion | flops 1313095680 | bytes 2163584 | tf_op jit(solution)/shard_map/conv_general_dilated | solution.py:13
  152.9 0.9 copy.24
  (25 shorter events, 0.1 us)
Async XLA Ops:
  0.0 149.5 %copy-start = (bf16[3,3,256,256]{3,2,1,0:T(8,128)(2,1)S(1)}, bf16[3,3,256,256]{3,2,1,0:T(8,128)(2,1)}, u32[]{:S(2)}) copy-start(bf16[3,3,256,256]{3,2,1,0:T(8,128)(2,1)} %param.18) | copy-start | bytes 3538948
  0.0 8.4 %copy-start.3 = (s32[128,1]{0,1:T(1,128)S(1)}, s32[128,1]{0,1:T(1,128)}, u32[]{:S(2)}) copy-start(s32[128,1]{0,1:T(1,128)} %param.14) | copy-start | bytes 1540
  0.0 10.7 %copy-start.7 = (s32[128]{0:T(128)S(1)}, s32[128]{0:T(128)}, u32[]{:S(2)}) copy-start(s32[128]{0:T(128)} %param.12) | copy-start | bytes 1540
  3.2 23.4 %all-to-all-start.1 = ((bf16[1,73,64,128]{3,1,0,2:T(8,128)(2,1)}), bf16[1,73,64,128]{3,1,0,2:T(8,128)(2,1)S(1)}, u32[]{:S(2)}, u32[]{:S(2)}) async-start(bf16[1,73,64,128]{3,1,0,2:T(8,128)(2,1)} %copy.18), calls=%async_computation.1 | async-start | bytes 2621440 | tf_op jit(solution)/shard_map/all_to_all | solution.py:36
  26.6 10.3 %all-to-all-start.3 = ((s32[8,1,24]{2,1,0:T(1,128)}), s32[8,1,24]{2,1,0:T(1,128)S(1)}, u32[]{:S(2)}, u32[]{:S(2)}) async-start(s32[8,1,24]{2,1,0:T(1,128)} %all_to_all.36), calls=%async_computation.3 | async-start | bytes 8192 | tf_op jit(solution)/shard_map/all_to_all | solution.py:63
  36.9 23.9 %all-to-all-start = ((s32[8,1,24]{2,1,0:T(1,128)}), s32[8,1,24]{2,1,0:T(1,128)S(1)}, u32[]{:S(2)}, u32[]{:S(2)}) async-start(s32[8,1,24]{2,1,0:T(1,128)} %all_to_all.30), calls=%async_computation | async-start | bytes 8192 | tf_op jit(solution)/shard_map/all_to_all | solution.py:64
  42.7 2.4 %copy-start.2 = (bf16[128,73,64]{1,2,0:T(8,128)(2,1)S(1)}, bf16[128,73,64]{1,2,0:T(8,128)(2,1)}, u32[]{:S(2)}) copy-start(bf16[128,73,64]{1,2,0:T(8,128)(2,1)} %fusion.4) | copy-start | bytes 3588100
  60.8 6.1 %copy-start.1 = (bf16[16,64,144]{2,1,0:T(8,128)(2,1)S(1)}, bf16[16,64,144]{2,1,0:T(8,128)(2,1)}, u32[]{:S(2)}) copy-start(bf16[16,64,144]{2,1,0:T(8,128)(2,1)} %param.11) | copy-start | bytes 884740
  60.8 42.7 %all-to-all-start.2 = ((bf16[8,24,1,73,64]{3,4,1,2,0:T(8,128)(2,1)}), bf16[8,24,1,73,64]{3,4,1,2,0:T(8,128)(2,1)}, u32[]{:S(2)}, u32[]{:S(2)}) async-start(bf16[8,24,1,73,64]{3,4,1,2,0:T(8,128)(2,1)} %bitcast.39), calls=%async_computation.2 | async-start | bytes 6291456 | tf_op jit(solution)/shard_map/all_to_all | solution.py:62
  143.4 6.2 %copy-start.4 = (bf16[3,3,73,256]{3,2,1,0:T(8,128)(2,1)S(1)}, bf16[3,3,73,256]{3,2,1,0:T(8,128)(2,1)}, u32[]{:S(2)}) copy-start(bf16[3,3,73,256]{3,2,1,0:T(8,128)(2,1)} %param.16) | copy-start | bytes 1009156
  143.4 6.2 %copy-start.5 = (f32[256]{0:T(256)S(1)}, f32[256]{0:T(256)}, u32[]{:S(2)}) copy-start(f32[256]{0:T(256)} %param.17) | copy-start | bytes 3076
  143.4 6.2 %copy-start.6 = (f32[256]{0:T(256)S(1)}, f32[256]{0:T(256)}, u32[]{:S(2)}) copy-start(f32[256]{0:T(256)} %param.19) | copy-start | bytes 3076
where the time goes:
time: 155 us; the launch traced here: 154 us
  local copies, waits for them, and re-layouts  73.3 us (47%)
  waiting for transfers between devices  44.4 us (29%)
  starting transfers between devices  17.4 us (11%)
  matrix products  15.7 us (10%)
  other arithmetic  2.75 us (2%)
    all_to_all x1, waiting for transfers between devices, per_device(): lax.all_to_all(outgoing, 'space', split_axis=0, concat_axis=0, tiled=True)  28.5 us
    all_to_all x1, waiting for transfers between devices, per_device(): lax.all_to_all(frames, 'space', split_axis=2, concat_axis=3, tiled=True)  15.9 us
    scatter x1, local copies, waits for them, and re-layouts, per_device(): jnp.zeros((flat_count, local_times, variables, SB), jnp.bfloat16).at[places]  15.7 us
    reshape x1, local copies, waits for them, and re-layouts, per_device(): partial_value.reshape(flat_count, -1)  12.1 us
    convert_element_type x1, local copies, waits for them, and re-layouts, per_device(): partial_value = jnp.einsum('nktvs,nksc->nktvc', rows_part, matrices, pref...  10.9 us
    reshape x2, local copies, waits for them, and re-layouts, per_device(): summed.astype(jnp.bfloat16)  10.6 us
    dot_general x1, matrix products, per_device(): jnp.einsum('nktvs,nksc->nktvc', rows_part, matrices, preferred_element_ty...  9.61 us
    gather x1, local copies, waits for them, and re-layouts, per_device(): matrices = jnp.take(regrid_mats, matrix_part, axis=0)  8.06 us
  transfers between devices with their start and end apart: 4, of which 2 were waited for; matrix products, arithmetic and copies ran while one was open for 24% of the time, Pallas kernels for 0%

commit v1 on v0

--- a/solution.py
+++ b/solution.py
@@ -1,12 +1,310 @@
+import functools
+
 import jax
 import jax.numpy as jnp
 from jax import lax
+from jax.experimental import pallas as pl
+from jax.experimental.pallas import tpu as pltpu
 from jax.sharding import PartitionSpec as P
 
 SIDE = 8
 SB = 64
 BLK_DEV = 12
 PAD_SIDE = 12
+
+MESH = pl.DeviceIdType.MESH
+VMEM = pl.BlockSpec(memory_space=pltpu.VMEM)
+LANES = 128
+ROW = 16
+GROUP = 4
+CHUNKS = 3
+MATCH = 1 << 20
+
+
+def greet(peers):
+    barrier = pltpu.get_barrier_semaphore()
+    for peer in peers:
+        pl.semaphore_signal(barrier, inc=1, device_id={"space": peer}, device_id_type=MESH)
+    pl.semaphore_wait(barrier, len(peers))
+
+
+def table_kernel(devices, table_ref, all_ref, send_sem, recv_sem):
+    me = lax.axis_index("space")
+    greet([lax.rem(me + step, devices) for step in range(1, devices)])
+    copies = []
+    for step in range(1, devices):
+        copy = pltpu.make_async_remote_copy(
+            src_ref=table_ref,
+            dst_ref=all_ref.at[me],
+            send_sem=send_sem.at[step],
+            recv_sem=recv_sem.at[step],
+            device_id={"space": lax.rem(me + step, devices)},
+            device_id_type=MESH,
+        )
+        copy.start()
+        copies.append(copy)
+    all_ref[me] = table_ref[...]
+    for copy in copies:
+        copy.wait()
+
+
+def gather_tables(table, devices):
+    return pl.pallas_call(
+        functools.partial(table_kernel, devices),
+        out_shape=jax.ShapeDtypeStruct((devices,) + table.shape, table.dtype),
+        in_specs=[VMEM],
+        out_specs=VMEM,
+        scratch_shapes=[
+            pltpu.SemaphoreType.DMA((devices,)),
+            pltpu.SemaphoreType.DMA((devices,)),
+        ],
+        compiler_params=pltpu.CompilerParams(collective_id=0, has_side_effects=True),
+        name="pair_tables",
+    )(table)
+
+
+def regrid_kernel(
+    strip_blocks, row_blocks, table_ref, frames_ref, mats_ref, out_ref,
+    wide, total, words_v, words_s, chosen, sem,
+):
+    devices, _, pairs = table_ref.shape
+    variables, lats, lanes = frames_ref.shape
+    padded = wide.shape[0] // lats
+    blocks = out_ref.shape[0]
+    me = lax.axis_index("space")
+    source = table_ref[:, 0, :]
+    matrix = table_ref[:, 1, :]
+    target = table_ref[:, 2, :] * BLK_DEV + table_ref[:, 3, :]
+    band = lax.broadcasted_iota(jnp.int32, (devices, pairs), 0)
+    lat = band * (lats // devices) + source // row_blocks
+    place = source % row_blocks
+    mine = (place // strip_blocks) == me
+    word = target * 2048 + lat * 32 + matrix * strip_blocks + place % strip_blocks
+    words_v[...] = word + jnp.where(mine, MATCH, 0)
+    move = pltpu.make_async_copy(words_v, words_s, sem)
+    move.start()
+
+    wide[pl.ds(variables * lats, (padded - variables) * lats), :] = jnp.zeros(
+        ((padded - variables) * lats, lanes), jnp.float32
+    )
+
+    @pl.loop(0, variables)
+    def _(v):
+        wide[pl.ds(pl.multiple_of(v * lats, lats), lats), :] = frames_ref[v].astype(jnp.float32)
+
+    @pl.loop(0, blocks + 1)
+    def _(b):
+        total[b] = jnp.zeros(total.shape[1:], jnp.float32)
+
+    move.wait()
+
+    def scan_row(row, count):
+        def scan(step, count):
+            for lane in range(8):
+                value = words_s[row, step * 8 + lane]
+                chosen[count] = value
+                count = count + (value >> 20)
+            return count
+
+        return lax.fori_loop(0, pairs // 8, scan, count)
+
+    count = lax.fori_loop(0, devices, scan_row, 0)
+    for extra in range(GROUP):
+        chosen[count + extra] = blocks * 2048
+
+    @pl.loop(0, (count + GROUP - 1) // GROUP)
+    def _(step):
+        products, homes = [], []
+        for lane in range(GROUP):
+            value = chosen[step * GROUP + lane] & (MATCH - 1)
+            homes.append(value >> 11)
+            cells = wide[pl.ds((value >> 5) & 63, padded, stride=lats), :].astype(jnp.bfloat16)
+            products.append(
+                lax.dot_general(
+                    mats_ref[value & 31], cells, (((1,), (1,)), ((), ())),
+                    preferred_element_type=jnp.float32,
+                )
+            )
+        for home, product in zip(homes, products):
+            total[home, :, :padded] += product
+
+    @pl.loop(0, blocks)
+    def _(b):
+        out_ref[b] = total[b].astype(jnp.bfloat16)
+
+
+def regrid(tables, frames, mats, blocks, strip_blocks, row_blocks):
+    devices, _, pairs = tables.shape
+    variables, lats, lanes = frames.shape
+    padded = -(-variables // 16) * 16
+    cells = mats.shape[1]
+    return pl.pallas_call(
+        functools.partial(regrid_kernel, strip_blocks, row_blocks),
+        out_shape=jax.ShapeDtypeStruct((blocks, cells, LANES), jnp.bfloat16),
+        in_specs=[VMEM] * 3,
+        out_specs=VMEM,
+        scratch_shapes=[
+            pltpu.VMEM((padded * lats, lanes), jnp.float32),
+            pltpu.VMEM((blocks + 1, cells, LANES), jnp.float32),
+            pltpu.VMEM((devices, pairs), jnp.int32),
+            pltpu.SMEM((devices, pairs), jnp.int32),
+            pltpu.SMEM((devices * pairs + 8,), jnp.int32),
+            pltpu.SemaphoreType.DMA,
+        ],
+        compiler_params=pltpu.CompilerParams(vmem_limit_bytes=40 << 20),
+        name="regrid_pairs",
+    )(tables, frames, mats)
+
+
+def encode_kernel(
+    chips, part_ref, w1_ref, b1_ref, w2_ref, b2_ref, out_ref,
+    near, sums, far, flat, wide, hid, taps,
+    near_send, near_recv, far_send, far_recv,
+):
+    me = lax.axis_index("space")
+    chip, core = me // 2, lax.rem(me, 2)
+    size = BLK_DEV // CHUNKS
+    cells = part_ref.shape[1]
+    order = list(range(1, chips)) + [0]
+    peers = [lax.rem(chip + step, chips) for step in range(chips)]
+    sibling = chip * 2 + 1 - core
+    greet([sibling] + [peers[step] * 2 + core for step in range(1, chips)])
+
+    near_copies = {}
+    for chunk in range(CHUNKS):
+        for step in order:
+            first = (peers[step] * 2 + 1 - core) * BLK_DEV + chunk * size
+            copy = pltpu.make_async_remote_copy(
+                src_ref=part_ref.at[pl.ds(first, size)],
+                dst_ref=near.at[step, pl.ds(chunk * size, size)],
+                send_sem=near_send.at[chunk, step],
+                recv_sem=near_recv.at[chunk, step],
+                device_id={"space": sibling},
+                device_id_type=MESH,
+            )
+            copy.start()
+            near_copies[chunk, step] = copy
+
+    far_copies = {}
+    for chunk in range(CHUNKS):
+        for step in order:
+            near_copies[chunk, step].wait_recv()
+            first = (peers[step] * 2 + core) * BLK_DEV + chunk * size
+            here = pl.ds(chunk * size, size)
+            sums[step, here] = (
+                part_ref[pl.ds(first, size)].astype(jnp.float32)
+                + near[step, here].astype(jnp.float32)
+            ).astype(jnp.bfloat16)
+            if step:
+                copy = pltpu.make_async_remote_copy(
+                    src_ref=sums.at[step, here],
+                    dst_ref=far.at[step - 1, here],
+                    send_sem=far_send.at[chunk, step],
+                    recv_sem=far_recv.at[chunk, step],
+                    device_id={"space": peers[step] * 2 + core},
+                    device_id_type=MESH,
+                )
+                copy.start()
+                far_copies[chunk, step] = copy
+
+    side = PAD_SIDE
+    mid = side - 2
+    last = side - 4
+    for chunk in range(CHUNKS):
+        here = pl.ds(chunk * size, size)
+        for step in range(1, chips):
+            far_copies[chunk, step].wait_recv()
+        for b in range(size):
+            field = sums[0, chunk * size + b].astype(jnp.float32)
+            for step in range(1, chips):
+                field = field + far[step - 1, chunk * size + b].astype(jnp.float32)
+            flat[pl.ds(0, cells), :] = field
+            for i in range(side):
+                for c in range(3):
+                    wide[b, i, :, c * LANES:(c + 1) * LANES] = flat[
+                        pl.ds(i * side + c, ROW), :
+                    ].astype(jnp.bfloat16)
+        first_out = b1_ref[...]
+        for a in range(3):
+            rows = wide[:, a:a + mid].reshape(size * mid * ROW, 3 * LANES)
+            first_out = first_out + jnp.dot(rows, w1_ref[a], preferred_element_type=jnp.float32)
+        hid[pl.ds(0, size * mid * ROW), :] = jax.nn.gelu(first_out, approximate=True)
+        channels = hid.shape[1]
+        for c in range(3):
+            taps[:, c * channels:(c + 1) * channels] = hid[
+                pl.ds(c, size * mid * ROW), :
+            ].astype(jnp.bfloat16)
+        shifted = taps[...].reshape(size, mid, ROW, 3 * channels)
+        second = b2_ref[...]
+        for a in range(3):
+            rows = shifted[:, a:a + last].reshape(size * last * ROW, 3 * channels)
+            second = second + jnp.dot(rows, w2_ref[a], preferred_element_type=jnp.float32)
+        second = second.reshape(size, last, ROW, -1)[:, :, :last, :]
+        out_ref[here] = second.reshape(size, last * last, -1).astype(jnp.bfloat16)
+
+    for copy in list(near_copies.values()) + list(far_copies.values()):
+        copy.wait_send()
+
+
+def encode(part, w1, b1, w2, b2, chips):
+    cells = part.shape[1]
+    channels = w2.shape[-1]
+    hidden = w1.shape[-1]
+    size = BLK_DEV // CHUNKS
+    rows = size * (PAD_SIDE - 2) * ROW
+    semaphores = [pltpu.SemaphoreType.DMA((CHUNKS, chips))] * 4
+    return pl.pallas_call(
+        functools.partial(encode_kernel, chips),
+        out_shape=jax.ShapeDtypeStruct((BLK_DEV, SIDE * SIDE, channels), jnp.bfloat16),
+        in_specs=[VMEM] * 5,
+        out_specs=VMEM,
+        scratch_shapes=[
+            pltpu.VMEM((chips, BLK_DEV, cells, LANES), jnp.bfloat16),
+            pltpu.VMEM((chips, BLK_DEV, cells, LANES), jnp.bfloat16),
+            pltpu.VMEM((chips - 1, BLK_DEV, cells, LANES), jnp.bfloat16),
+            pltpu.VMEM((cells + ROW, LANES), jnp.float32),
+            pltpu.VMEM((size, PAD_SIDE, ROW, 3 * LANES), jnp.bfloat16),
+            pltpu.VMEM((rows + ROW, hidden), jnp.float32),
+            pltpu.VMEM((rows, 3 * hidden), jnp.bfloat16),
+        ] + semaphores,
+        compiler_params=pltpu.CompilerParams(
+            collective_id=1, has_side_effects=True, vmem_limit_bytes=40 << 20
+        ),
+        name="reduce_and_encode",
+    )(part, w1, b1, w2, b2)
+
+
+def strips(
+    frames,
+    regrid_mats,
+    pair_source,
+    pair_matrix,
+    pair_device,
+    pair_local,
+    w_first,
+    b_first,
+    w_second,
+    b_second,
+):
+    devices = lax.axis_size("space")
+    strip_blocks = frames.shape[3] // SB
+    row_blocks = strip_blocks * devices
+    table = jnp.stack([pair_source, pair_matrix, pair_device[:, 0], pair_local])
+    tables = gather_tables(table, devices)
+    turned = jnp.transpose(regrid_mats, (0, 2, 1))
+    mats = jnp.stack(
+        [
+            jnp.pad(turned, ((0, 0), (0, 0), (place * SB, (strip_blocks - 1 - place) * SB)))
+            for place in range(strip_blocks)
+        ],
+        axis=1,
+    ).reshape(-1, turned.shape[1], strip_blocks * SB)
+    part = regrid(tables, frames[0], mats, devices * BLK_DEV, strip_blocks, row_blocks)
+    lift = LANES - w_first.shape[2]
+    w1 = jnp.pad(w_first, ((0, 0), (0, 0), (0, lift), (0, 0))).reshape(3, 3 * LANES, -1)
+    w2 = w_second.reshape(3, -1, w_second.shape[-1])
+    out = encode(part, w1, b_first[None], w2, b_second[None], devices // 2)
+    return out[None]
 
 
 def conv_valid(inputs, weights, layout):
@@ -96,6 +394,14 @@
         P(),
     )
     out_specs = P("tm", "space", None, None)
-    return jax.shard_map(
-        per_device, mesh=mesh, in_specs=in_specs, out_specs=out_specs, check_vma=False
-    )
+    devices = mesh.shape["space"]
+
+    def program(frames, *rest):
+        local = (frames.shape[0] // mesh.shape["tm"], frames.shape[3] // devices)
+        whole_blocks = local == (1, LANES) and LANES % SB == 0 and devices % 2 == 0
+        body = strips if whole_blocks and frames.shape[2] <= SB else per_device
+        return jax.shard_map(
+            body, mesh=mesh, in_specs=in_specs, out_specs=out_specs, check_vma=False
+        )(frames, *rest)
+
+    return program

time: 155 us -> 61.3 us (0.40)
  local copies, waits for them, and re-layouts: 73.3 us -> 6.34 us
  Pallas kernels: 0 us -> 52.6 us
  waiting for transfers between devices: 44.4 us -> 0 us
  starting transfers between devices: 17.4 us -> 0 us
  matrix products: 15.7 us -> 0 us
    pallas_call x0 -> x3, Pallas kernels: none -> 52.6 us  [the longest x1 26.4 us: encode(): pl.pallas_call(functools.partial(encode_kernel, chips), out_shape=jax.Sha...]
    all_to_all x4 -> x0, waiting for transfers between devices: 44.4 us -> none  [the longest x1 28.5 us: per_device(): lax.all_to_all(outgoing, 'space', split_axis=0, concat_axis=0, tiled=True)]
    reshape x4 -> x0, local copies, waits for them, and re-layouts: 25.3 us -> none  [the longest x1 12.1 us: per_device(): partial_value.reshape(flat_count, -1)]
    scatter x3 -> x0, local copies, waits for them, and re-layouts: 17.9 us -> none  [the longest x1 15.7 us: per_device(): jnp.zeros((flat_count, local_times, variables, SB), jnp.bfloat16).at[places]]
    all_to_all x4 -> x0, starting transfers between devices: 17.4 us -> none  [the longest x1 5.17 us: per_device(): lax.all_to_all(frames, 'space', split_axis=2, concat_axis=3, tiled=True)]
    dot_general x2 -> x0, matrix products: 12.4 us -> none  [the longest x1 9.61 us: per_device(): jnp.einsum('nktvs,nksc->nktvc', rows_part, matrices, preferred_element_ty...]
    convert_element_type x1 -> x0, local copies, waits for them, and re-layouts: 10.9 us -> none  [per_device(): partial_value = jnp.einsum('nktvs,nksc->nktvc', rows_part, matrices, pref...]
    gather x2 -> x0, local copies, waits for them, and re-layouts: 10.6 us -> none  [the longest x1 8.06 us: per_device(): matrices = jnp.take(regrid_mats, matrix_part, axis=0)]
  transfers between devices with their start and end apart: 4 -> 0, of which waited for: 2 -> 0; matrix products, arithmetic and copies ran while one was open for 24% -> 0% of each run, Pallas kernels for 0% -> 0%
where the time goes in v1:
time: 61.3 us; the launch traced here: 61.4 us
  Pallas kernels  52.6 us (86%)
  local copies, waits for them, and re-layouts  6.34 us (10%)
  other arithmetic  2.33 us (4%)
    pallas_call x1, Pallas kernels, encode(): pl.pallas_call(functools.partial(encode_kernel, chips), out_shape=jax.Sha...  26.4 us
    pallas_call x1, Pallas kernels, regrid(): pl.pallas_call(functools.partial(regrid_kernel, strip_blocks, row_blocks)...  18.7 us
    pallas_call x1, Pallas kernels, gather_tables(): pl.pallas_call(functools.partial(table_kernel, devices), out_shape=jax.Sh...  7.5 us
    another operation x2, local copies, waits for them, and re-layouts, strips(): jnp.stack([jnp.pad(turned, ((0, 0), (0, 0), (place * SB, (strip_blocks -...  4.8 us
    another operation x1, other arithmetic, strips(): jnp.stack([jnp.pad(turned, ((0, 0), (0, 0), (place * SB, (strip_blocks -...  1.74 us
    unnamed x21, local copies, waits for them, and re-layouts  1.49 us

profile of v1, /device:TPU:0, one launch (start us, length us, event | category | flops | bytes accessed | tf_op | source)
XLA Modules:
  0.0 61.4 jit_solution(6839654132472506439)
XLA Ops:
  0.0 1.6 %pad_bitcast_fusion.1 = (bf16[16,1,144,128]{2,3,0,1:T(8,128)(2,1)S(1)}, bf16[16,1,144,128]{2,3,0,1:T(8,128)(2,1)S(1)}) fusion(bf16[16,144,64]{1,2,0:T(8,128)(2,1)} %bitcast.23), kind=kLoop, calls=%fused_computation.2 | loop fusion | bytes 1474560 | tf_op jit(solution)/shard_map/stack | solution.py:295
  1.6 1.7 %pad_maximum_fusion = bf16[16,2,144,128]{2,3,0,1:T(8,128)(2,1)} fusion(bf16[16,1,144,128]{2,3,0,1:T(8,128)(2,1)S(1)} %get-tuple-element.6, bf16[16,1,144,128]{2,3,0,1:T(8,128)(2,1)S(1)} %get-tuple-element.5), kind=kLoop, calls=%fused_computation | loop fusion | flops 589824 | bytes 2359296 | tf_op jit(solution)/shard_map/stack | solution.py:295
  3.3 0.0 copy-start.6
  3.3 0.0 copy-start.7
  3.3 0.0 copy-start.8
  3.3 0.0 copy-start.9
  3.3 0.0 copy-start
  3.4 3.2 %copy.11 = bf16[16,2,144,128]{3,2,1,0:T(8,128)(2,1)S(1)} copy(bf16[16,2,144,128]{2,3,0,1:T(8,128)(2,1)} %pad_maximum_fusion) | data formatting | bytes 2359296 | tf_op jit(solution)/shard_map/stack | solution.py:295
  6.6 0.0 copy-done.6
  6.6 0.0 copy-done.7
  6.6 0.0 copy-done.8
  6.6 0.0 copy-done.9
  6.6 0.6 pad_add_fusion.table_ref
  7.2 7.5 %pair_tables.1.table_ref = s32[8,4,128]{2,1,0:T(4,128)} custom-call(s32[4,128]{1,0:T(4,128)} %pad_add_fusion.table_ref), custom_call_target="tpu_custom_call" | custom-call | tf_op jit(solution)/shard_map/pair_tables/pallas_call | solution.py:52
  14.7 0.0 copy-done
  14.7 0.0 copy-start.2
  14.7 0.7 %copy-done.2 = s32[8,4,128]{2,1,0:T(4,128)S(1)} copy-done((s32[8,4,128]{2,1,0:T(4,128)S(1)}, s32[8,4,128]{2,1,0:T(4,128)}, u32[]{:S(2)}) %copy-start.2) | copy-done | bytes 16408
  15.4 0.0 copy-start.5
  15.4 0.0 copy-start.1
  15.4 0.0 copy-start.3
  15.4 0.0 copy-start.4
  15.5 18.7 %regrid_pairs.1.part_ref = bf16[96,144,128]{2,1,0:T(8,128)(2,1)S(1)} custom-call(s32[8,4,128]{2,1,0:T(4,128)S(1)} %copy-done.2, bf16[73,64,128]{2,1,0:T(8,128)(2,1)S(1)} %bitcast.19, bf16[32,144,128]{2,1,0:T(8,128)(2,1)S(1)} %bitcast.16), custom_call_target="tpu_custom_call" | custom-call | tf_op jit(solution)/shard_map/regrid_pairs/pallas_call | solution.py:141
  34.2 0.0 copy-done.5
  34.2 0.0 copy-done.1
  34.3 0.0 copy-done.3
  34.3 0.0 copy-done.4
  34.3 26.4 %reduce_and_encode.1 = bf16[12,64,256]{2,1,0:T(8,128)(2,1)S(1)} custom-call(bf16[96,144,128]{2,1,0:T(8,128)(2,1)S(1)} %regrid_pairs.1.part_ref, bf16[3,384,256]{2,1,0:T(8,128)(2,1)S(1)} %bitcast.17, f32[1,256]{1,0:T(1,128)S(1)} %bitcast.21, bf16[3,768,256]{2,1,0:T(8,128)(2,1)S(1)} %bitcast.20, f32[1,256]{1,0:T(1,128)S(1)} %bitcast.22), custom_call_target="tpu_custom_call" | custom-call | tf_op jit(solution)/shard_map/reduce_and_encode/pallas_call | solution.py:256
  60.7 0.7 %copy.13 = bf16[1,12,64,256]{3,2,1,0:T(8,128)(2,1)} copy(bf16[1,12,64,256]{3,2,1,0:T(8,128)(2,1)S(1)} %bitcast.18) | data formatting | bytes 786432
  (1 shorter events, 0.0 us)
Async XLA Ops:
  3.3 3.2 %copy-start.6 = (s32[128]{0:T(128)S(1)}, s32[128]{0:T(128)}, u32[]{:S(2)}) copy-start(s32[128]{0:T(128)} %param.15) | copy-start | bytes 1540
  3.3 3.3 %copy-start.7 = (s32[128,1]{0,1:T(1,128)S(1)}, s32[128,1]{0,1:T(1,128)}, u32[]{:S(2)}) copy-start(s32[128,1]{0,1:T(1,128)} %param.14) | copy-start | bytes 1540
  3.3 3.3 %copy-start.8 = (s32[128]{0:T(128)S(1)}, s32[128]{0:T(128)}, u32[]{:S(2)}) copy-start(s32[128]{0:T(128)} %param.13) | copy-start | bytes 1540
  3.3 3.3 %copy-start.9 = (s32[128]{0:T(128)S(1)}, s32[128]{0:T(128)}, u32[]{:S(2)}) copy-start(s32[128]{0:T(128)} %param.12) | copy-start | bytes 1540
  3.3 11.4 %copy-start = (bf16[1,73,64,128]{3,2,1,0:T(8,128)(2,1)S(1)}, bf16[1,73,64,128]{3,2,1,0:T(8,128)(2,1)}, u32[]{:S(2)}) copy-start(bf16[1,73,64,128]{3,2,1,0:T(8,128)(2,1)} %param.10) | copy-start | bytes 3588100
  14.7 0.7 %copy-start.2 = (s32[8,4,128]{2,1,0:T(4,128)S(1)}, s32[8,4,128]{2,1,0:T(4,128)}, u32[]{:S(2)}) copy-start(s32[8,4,128]{2,1,0:T(4,128)} %pair_tables.1.table_ref) | copy-start | bytes 49156
  15.4 18.7 %copy-start.5 = (bf16[3,3,73,256]{3,2,1,0:T(8,128)(2,1)S(1)}, bf16[3,3,73,256]{3,2,1,0:T(8,128)(2,1)}, u32[]{:S(2)}) copy-start(bf16[3,3,73,256]{3,2,1,0:T(8,128)(2,1)} %param.16) | copy-start | bytes 1009156
  15.4 18.8 %copy-start.1 = (bf16[3,3,256,256]{3,2,1,0:T(8,128)(2,1)S(1)}, bf16[3,3,256,256]{3,2,1,0:T(8,128)(2,1)}, u32[]{:S(2)}) copy-start(bf16[3,3,256,256]{3,2,1,0:T(8,128)(2,1)} %param.18) | copy-start | bytes 3538948
  15.4 18.8 %copy-start.3 = (f32[256]{0:T(256)S(1)}, f32[256]{0:T(256)}, u32[]{:S(2)}) copy-start(f32[256]{0:T(256)} %param.17) | copy-start | bytes 3076
  15.4 18.8 %copy-start.4 = (f32[256]{0:T(256)S(1)}, f32[256]{0:T(256)}, u32[]{:S(2)}) copy-start(f32[256]{0:T(256)} %param.19) | copy-start | bytes 3076

commit v2 on v1

--- a/solution.py
+++ b/solution.py
@@ -19,6 +19,8 @@
 GROUP = 4
 CHUNKS = 3
 MATCH = 1 << 20
+FRONT = 64
+TAIL = 16
 
 
 def greet(peers):
@@ -28,7 +30,7 @@
     pl.semaphore_wait(barrier, len(peers))
 
 
-def table_kernel(devices, table_ref, all_ref, send_sem, recv_sem):
+def table_kernel(devices, table_ref, mats_ref, all_ref, turned_ref, send_sem, recv_sem):
     me = lax.axis_index("space")
     greet([lax.rem(me + step, devices) for step in range(1, devices)])
     copies = []
@@ -44,23 +46,39 @@
         copy.start()
         copies.append(copy)
     all_ref[me] = table_ref[...]
+    strip_blocks = turned_ref.shape[0] // mats_ref.shape[0]
+
+    @pl.loop(0, mats_ref.shape[0])
+    def _(m):
+        matrix = mats_ref[m].astype(jnp.float32)
+        blank = jnp.zeros_like(matrix)
+        for place in range(strip_blocks):
+            stack = [matrix if other == place else blank for other in range(strip_blocks)]
+            turned_ref[m * strip_blocks + place] = (
+                jnp.concatenate(stack, axis=0).T.astype(jnp.bfloat16)
+            )
+
     for copy in copies:
         copy.wait()
 
 
-def gather_tables(table, devices):
+def gather_tables(table, mats, devices, strip_blocks):
+    turned = (mats.shape[0] * strip_blocks, mats.shape[2], strip_blocks * mats.shape[1])
     return pl.pallas_call(
         functools.partial(table_kernel, devices),
-        out_shape=jax.ShapeDtypeStruct((devices,) + table.shape, table.dtype),
-        in_specs=[VMEM],
-        out_specs=VMEM,
+        out_shape=(
+            jax.ShapeDtypeStruct((devices,) + table.shape, table.dtype),
+            jax.ShapeDtypeStruct(turned, mats.dtype),
+        ),
+        in_specs=[VMEM] * 2,
+        out_specs=(VMEM, VMEM),
         scratch_shapes=[
             pltpu.SemaphoreType.DMA((devices,)),
             pltpu.SemaphoreType.DMA((devices,)),
         ],
-        compiler_params=pltpu.CompilerParams(collective_id=0, has_side_effects=True),
+        compiler_params=pltpu.CompilerParams(collective_id=0, has_side_effects=True, vmem_limit_bytes=16 << 20),
         name="pair_tables",
-    )(table)
+    )(table, mats)
 
 
 def regrid_kernel(
@@ -100,13 +118,15 @@
 
     def scan_row(row, count):
         def scan(step, count):
-            for lane in range(8):
-                value = words_s[row, step * 8 + lane]
-                chosen[count] = value
-                count = count + (value >> 20)
-            return count
-
-        return lax.fori_loop(0, pairs // 8, scan, count)
+            values = [words_s[row, step * 16 + lane] for lane in range(16)]
+            places = [count]
+            for value in values:
+                places.append(places[-1] + (value >> 20))
+            for value, place in zip(values, places):
+                chosen[place] = value
+            return places[-1]
+
+        return lax.fori_loop(0, pairs // 16, scan, count)
 
     count = lax.fori_loop(0, devices, scan_row, 0)
     for extra in range(GROUP):
@@ -156,9 +176,43 @@
     )(tables, frames, mats)
 
 
+def pack_fields(fields):
+    half = fields[0].shape[0] // 2
+    lane = lax.broadcasted_iota(jnp.int32, (half, LANES), 1)
+    rest = jnp.zeros((half, LANES), jnp.float32)
+    rows = []
+    for b, field in enumerate(fields):
+        upper, lower = field[:half], field[half:]
+        rows.append(jnp.where(lane < FRONT, upper, pltpu.roll(lower, FRONT, 1)))
+        for side, piece in enumerate((upper, lower)):
+            start = (2 * b + side) * TAIL
+            moved = pltpu.roll(piece, (start - FRONT) % LANES, 1)
+            rest = jnp.where((lane >= start) & (lane < start + TAIL), moved, rest)
+    rows.append(rest)
+    spare = -len(rows) * half % ROW
+    if spare:
+        rows.append(jnp.zeros((spare, LANES), jnp.float32))
+    return jnp.concatenate(rows, axis=0)
+
+
+def unpack_field(packed, b, size, cells):
+    half = cells // 2
+    lane = lax.broadcasted_iota(jnp.int32, (half, LANES), 1)
+    front = packed[b * half:(b + 1) * half]
+    rest = packed[size * half:(size + 1) * half]
+    pieces = []
+    for side in range(2):
+        start = (2 * b + side) * TAIL
+        head = pltpu.roll(front, FRONT, 1) if side else front
+        tail = pltpu.roll(rest, (FRONT - start) % LANES, 1)
+        tail = jnp.where(lane < FRONT + TAIL, tail, 0.0)
+        pieces.append(jnp.where(lane < FRONT, head, tail))
+    return jnp.concatenate(pieces, axis=0)
+
+
 def encode_kernel(
     chips, part_ref, w1_ref, b1_ref, w2_ref, b2_ref, out_ref,
-    near, sums, far, flat, wide, hid, taps,
+    near, own, sums, far, flat, wide, hid, taps,
     near_send, near_recv, far_send, far_recv,
 ):
     me = lax.axis_index("space")
@@ -191,14 +245,19 @@
             near_copies[chunk, step].wait_recv()
             first = (peers[step] * 2 + core) * BLK_DEV + chunk * size
             here = pl.ds(chunk * size, size)
-            sums[step, here] = (
-                part_ref[pl.ds(first, size)].astype(jnp.float32)
-                + near[step, here].astype(jnp.float32)
-            ).astype(jnp.bfloat16)
-            if step:
+            fields = [
+                part_ref[first + b].astype(jnp.float32)
+                + near[step, chunk * size + b].astype(jnp.float32)
+                for b in range(size)
+            ]
+            if step == 0:
+                for b in range(size):
+                    own[chunk * size + b] = fields[b]
+            else:
+                sums[step - 1, chunk] = pack_fields(fields).astype(jnp.bfloat16)
                 copy = pltpu.make_async_remote_copy(
-                    src_ref=sums.at[step, here],
-                    dst_ref=far.at[step - 1, here],
+                    src_ref=sums.at[step - 1, chunk],
+                    dst_ref=far.at[step - 1, chunk],
                     send_sem=far_send.at[chunk, step],
                     recv_sem=far_recv.at[chunk, step],
                     device_id={"space": peers[step] * 2 + core},
@@ -214,11 +273,11 @@
         here = pl.ds(chunk * size, size)
         for step in range(1, chips):
             far_copies[chunk, step].wait_recv()
+        packed = far[0, chunk].astype(jnp.float32)
+        for step in range(1, chips - 1):
+            packed = packed + far[step, chunk].astype(jnp.float32)
         for b in range(size):
-            field = sums[0, chunk * size + b].astype(jnp.float32)
-            for step in range(1, chips):
-                field = field + far[step - 1, chunk * size + b].astype(jnp.float32)
-            flat[pl.ds(0, cells), :] = field
+            flat[pl.ds(0, cells), :] = own[chunk * size + b] + unpack_field(packed, b, size, cells)
             for i in range(side):
                 for c in range(3):
                     wide[b, i, :, c * LANES:(c + 1) * LANES] = flat[
@@ -252,6 +311,7 @@
     hidden = w1.shape[-1]
     size = BLK_DEV // CHUNKS
     rows = size * (PAD_SIDE - 2) * ROW
+    packed = -(-(size + 1) * (cells // 2) // ROW) * ROW
     semaphores = [pltpu.SemaphoreType.DMA((CHUNKS, chips))] * 4
     return pl.pallas_call(
         functools.partial(encode_kernel, chips),
@@ -260,8 +320,9 @@
         out_specs=VMEM,
         scratch_shapes=[
             pltpu.VMEM((chips, BLK_DEV, cells, LANES), jnp.bfloat16),
-            pltpu.VMEM((chips, BLK_DEV, cells, LANES), jnp.bfloat16),
-            pltpu.VMEM((chips - 1, BLK_DEV, cells, LANES), jnp.bfloat16),
+            pltpu.VMEM((BLK_DEV, cells, LANES), jnp.float32),
+            pltpu.VMEM((chips - 1, CHUNKS, packed, LANES), jnp.bfloat16),
+            pltpu.VMEM((chips - 1, CHUNKS, packed, LANES), jnp.bfloat16),
             pltpu.VMEM((cells + ROW, LANES), jnp.float32),
             pltpu.VMEM((size, PAD_SIDE, ROW, 3 * LANES), jnp.bfloat16),
             pltpu.VMEM((rows + ROW, hidden), jnp.float32),
@@ -290,15 +351,7 @@
     strip_blocks = frames.shape[3] // SB
     row_blocks = strip_blocks * devices
     table = jnp.stack([pair_source, pair_matrix, pair_device[:, 0], pair_local])
-    tables = gather_tables(table, devices)
-    turned = jnp.transpose(regrid_mats, (0, 2, 1))
-    mats = jnp.stack(
-        [
-            jnp.pad(turned, ((0, 0), (0, 0), (place * SB, (strip_blocks - 1 - place) * SB)))
-            for place in range(strip_blocks)
-        ],
-        axis=1,
-    ).reshape(-1, turned.shape[1], strip_blocks * SB)
+    tables, mats = gather_tables(table, regrid_mats, devices, strip_blocks)
     part = regrid(tables, frames[0], mats, devices * BLK_DEV, strip_blocks, row_blocks)
     lift = LANES - w_first.shape[2]
     w1 = jnp.pad(w_first, ((0, 0), (0, 0), (0, lift), (0, 0))).reshape(3, 3 * LANES, -1)
@@ -399,7 +452,8 @@
     def program(frames, *rest):
         local = (frames.shape[0] // mesh.shape["tm"], frames.shape[3] // devices)
         whole_blocks = local == (1, LANES) and LANES % SB == 0 and devices % 2 == 0
-        body = strips if whole_blocks and frames.shape[2] <= SB else per_device
+        fits = frames.shape[2] <= 64 and FRONT < frames.shape[1] <= FRONT + TAIL
+        body = strips if whole_blocks and fits else per_device
         return jax.shard_map(
             body, mesh=mesh, in_specs=in_specs, out_specs=out_specs, check_vma=False
         )(frames, *rest)

time: 61.3 us -> 48.9 us (0.80)
  Pallas kernels: 52.6 us -> 44.8 us
  local copies, waits for them, and re-layouts: 6.34 us -> 3.12 us
  other arithmetic: 2.33 us -> 0.71 us
    pallas_call x1, Pallas kernels: 26.4 us -> 20.8 us  [encode(): pl.pallas_call(functools.partial(encode_kernel, chips), out_shape=jax.Sha...]
    another operation x2 -> x0, local copies, waits for them, and re-layouts: 4.8 us -> none  [strips(): jnp.stack([jnp.pad(turned, ((0, 0), (0, 0), (place * SB, (strip_blocks -...]
    another operation x1 -> x0, other arithmetic: 1.74 us -> none  [strips(): jnp.stack([jnp.pad(turned, ((0, 0), (0, 0), (place * SB, (strip_blocks -...]
    unnamed x21 -> x13, local copies, waits for them, and re-layouts: 1.49 us -> 3.08 us
    pallas_call x1, Pallas kernels: 7.5 us -> 6.25 us  [gather_tables(): pl.pallas_call(functools.partial(table_kernel, devices), out_shape=(jax.S...]
    pallas_call x1, Pallas kernels: 18.7 us -> 17.7 us  [regrid(): pl.pallas_call(functools.partial(regrid_kernel, strip_blocks, row_blocks)...]
where the time goes in v2:
time: 48.9 us; the launch traced here: 48.7 us
  Pallas kernels  44.8 us (92%)
  local copies, waits for them, and re-layouts  3.12 us (6%)
  other arithmetic  0.71 us (1%)
    pallas_call x1, Pallas kernels, encode(): pl.pallas_call(functools.partial(encode_kernel, chips), out_shape=jax.Sha...  20.8 us
    pallas_call x1, Pallas kernels, regrid(): pl.pallas_call(functools.partial(regrid_kernel, strip_blocks, row_blocks)...  17.7 us
    pallas_call x1, Pallas kernels, gather_tables(): pl.pallas_call(functools.partial(table_kernel, devices), out_shape=(jax.S...  6.25 us
    unnamed x13, local copies, waits for them, and re-layouts  3.08 us

profile of v2, /device:TPU:0, one launch (start us, length us, event | category | flops | bytes accessed | tf_op | source)
XLA Modules:
  0.0 48.7 jit_solution(7661774896855678291)
XLA Ops:
  0.0 0.7 %pad_add_fusion.table_ref = s32[4,128]{1,0:T(4,128)S(1)} fusion(s32[1,128]{1,0:T(1,128)} %bitcast.16, s32[1,128]{1,0:T(1,128)} %bitcast.17, s32[1,128]{1,0:T(1,128)} %bitcast.18, s32[1,128]{1,0:T(1,128)} %bitcast.19), kind=kLoop, calls=%fused_computation | loop fusion | flops 1536 | bytes 4096 | tf_op jit(solution)/shard_map/stack | solution.py:353
  0.7 0.0 copy-start.2
  0.7 1.0 %copy-done.2 = bf16[16,64,144]{2,1,0:T(8,128)(2,1)S(1)} copy-done((bf16[16,64,144]{2,1,0:T(8,128)(2,1)S(1)}, bf16[16,64,144]{2,1,0:T(8,128)(2,1)}, u32[]{:S(2)}) %copy-start.2) | copy-done | bytes 294936
  1.8 6.3 %pair_tables.1 = (s32[8,4,128]{2,1,0:T(4,128)S(1)}, bf16[32,144,128]{2,1,0:T(8,128)(2,1)S(1)}) custom-call(s32[4,128]{1,0:T(4,128)S(1)} %pad_add_fusion.table_ref, bf16[16,64,144]{2,1,0:T(8,128)(2,1)S(1)} %copy-done.2), custom_call_target="tpu_custom_call" | custom-call | tf_op jit(solution)/shard_map/pair_tables/pallas_call | solution.py:67
  8.0 0.0 copy-start
  8.0 1.3 %copy-done = bf16[1,73,64,128]{3,2,1,0:T(8,128)(2,1)S(1)} copy-done((bf16[1,73,64,128]{3,2,1,0:T(8,128)(2,1)S(1)}, bf16[1,73,64,128]{3,2,1,0:T(8,128)(2,1)}, u32[]{:S(2)}) %copy-start) | copy-done | bytes 1196056
  9.3 0.0 copy-start.5
  9.3 0.0 copy-start.1
  9.3 0.0 copy-start.3
  9.3 0.0 copy-start.4
  9.3 17.7 %regrid_pairs.1.part_ref = bf16[96,144,128]{2,1,0:T(8,128)(2,1)S(1)} custom-call(s32[8,4,128]{2,1,0:T(4,128)S(1)} %get-tuple-element.7.table_ref, bf16[73,64,128]{2,1,0:T(8,128)(2,1)S(1)} %bitcast.12, bf16[32,144,128]{2,1,0:T(8,128)(2,1)S(1)} %get-tuple-element.8.mats_ref), custom_call_target="tpu_custom_call" | custom-call | tf_op jit(solution)/shard_map/regrid_pairs/pallas_call | solution.py:161
  27.1 0.0 copy-done.5
  27.1 0.0 copy-done.1
  27.1 0.0 copy-done.3
  27.1 0.0 copy-done.4
  27.2 20.8 %reduce_and_encode.1 = bf16[12,64,256]{2,1,0:T(8,128)(2,1)S(1)} custom-call(bf16[96,144,128]{2,1,0:T(8,128)(2,1)S(1)} %regrid_pairs.1.part_ref, bf16[3,384,256]{2,1,0:T(8,128)(2,1)S(1)} %bitcast.10, f32[1,256]{1,0:T(1,128)S(1)} %bitcast.14, bf16[3,768,256]{2,1,0:T(8,128)(2,1)S(1)} %bitcast.13, f32[1,256]{1,0:T(1,128)S(1)} %bitcast.15), custom_call_target="tpu_custom_call" | custom-call | tf_op jit(solution)/shard_map/reduce_and_encode/pallas_call | solution.py:316
  48.0 0.7 %copy.12 = bf16[1,12,64,256]{3,2,1,0:T(8,128)(2,1)} copy(bf16[1,12,64,256]{3,2,1,0:T(8,128)(2,1)S(1)} %bitcast.11) | data formatting | bytes 786432
  (1 shorter events, 0.0 us)
Async XLA Ops:
  0.7 1.0 %copy-start.2 = (bf16[16,64,144]{2,1,0:T(8,128)(2,1)S(1)}, bf16[16,64,144]{2,1,0:T(8,128)(2,1)}, u32[]{:S(2)}) copy-start(bf16[16,64,144]{2,1,0:T(8,128)(2,1)} %mats_ref.1) | copy-start | bytes 884740
  8.0 1.3 %copy-start = (bf16[1,73,64,128]{3,2,1,0:T(8,128)(2,1)S(1)}, bf16[1,73,64,128]{3,2,1,0:T(8,128)(2,1)}, u32[]{:S(2)}) copy-start(bf16[1,73,64,128]{3,2,1,0:T(8,128)(2,1)} %param.10) | copy-start | bytes 3588100
  9.3 17.8 %copy-start.5 = (bf16[3,3,73,256]{3,2,1,0:T(8,128)(2,1)S(1)}, bf16[3,3,73,256]{3,2,1,0:T(8,128)(2,1)}, u32[]{:S(2)}) copy-start(bf16[3,3,73,256]{3,2,1,0:T(8,128)(2,1)} %param.16) | copy-start | bytes 1009156
  9.3 17.8 %copy-start.1 = (bf16[3,3,256,256]{3,2,1,0:T(8,128)(2,1)S(1)}, bf16[3,3,256,256]{3,2,1,0:T(8,128)(2,1)}, u32[]{:S(2)}) copy-start(bf16[3,3,256,256]{3,2,1,0:T(8,128)(2,1)} %param.18) | copy-start | bytes 3538948
  9.3 17.8 %copy-start.3 = (f32[256]{0:T(256)S(1)}, f32[256]{0:T(256)}, u32[]{:S(2)}) copy-start(f32[256]{0:T(256)} %param.17) | copy-start | bytes 3076
  9.3 17.8 %copy-start.4 = (f32[256]{0:T(256)S(1)}, f32[256]{0:T(256)}, u32[]{:S(2)}) copy-start(f32[256]{0:T(256)} %param.19) | copy-start | bytes 3076

commit v3 on v2

--- a/solution.py
+++ b/solution.py
@@ -16,7 +16,7 @@
 VMEM = pl.BlockSpec(memory_space=pltpu.VMEM)
 LANES = 128
 ROW = 16
-GROUP = 4
+GROUP = 8
 CHUNKS = 3
 MATCH = 1 << 20
 FRONT = 64
@@ -30,9 +30,25 @@
     pl.semaphore_wait(barrier, len(peers))
 
 
-def table_kernel(devices, table_ref, mats_ref, all_ref, turned_ref, send_sem, recv_sem):
+def table_kernel(
+    devices, table_ref, mats_ref, frames_ref, all_ref, turned_ref, cells_ref, wide, send_sem, recv_sem
+):
     me = lax.axis_index("space")
-    greet([lax.rem(me + step, devices) for step in range(1, devices)])
+    barrier = pltpu.get_barrier_semaphore()
+    for step in range(1, devices):
+        peer = lax.rem(me + step, devices)
+        pl.semaphore_signal(barrier, inc=1, device_id={"space": peer}, device_id_type=MESH)
+    variables, lats, lanes = frames_ref.shape
+    padded = cells_ref.shape[1]
+    wide[pl.ds(variables * lats, (padded - variables) * lats), :] = jnp.zeros(
+        ((padded - variables) * lats, lanes), jnp.float32
+    )
+
+    @pl.loop(0, variables)
+    def _(v):
+        wide[pl.ds(pl.multiple_of(v * lats, lats), lats), :] = frames_ref[v].astype(jnp.float32)
+
+    pl.semaphore_wait(barrier, devices - 1)
     copies = []
     for step in range(1, devices):
         copy = pltpu.make_async_remote_copy(
@@ -58,36 +74,43 @@
                 jnp.concatenate(stack, axis=0).T.astype(jnp.bfloat16)
             )
 
+    @pl.loop(0, lats)
+    def _(lat):
+        cells_ref[lat] = wide[pl.ds(lat, padded, stride=lats), :].astype(jnp.bfloat16)
+
     for copy in copies:
         copy.wait()
 
 
-def gather_tables(table, mats, devices, strip_blocks):
+def gather_tables(table, mats, frames, devices, strip_blocks):
+    variables, lats, lanes = frames.shape
+    padded = -(-variables // 16) * 16
     turned = (mats.shape[0] * strip_blocks, mats.shape[2], strip_blocks * mats.shape[1])
     return pl.pallas_call(
         functools.partial(table_kernel, devices),
         out_shape=(
             jax.ShapeDtypeStruct((devices,) + table.shape, table.dtype),
             jax.ShapeDtypeStruct(turned, mats.dtype),
+            jax.ShapeDtypeStruct((lats, padded, lanes), frames.dtype),
         ),
-        in_specs=[VMEM] * 2,
-        out_specs=(VMEM, VMEM),
+        in_specs=[VMEM] * 3,
+        out_specs=(VMEM, VMEM, VMEM),
         scratch_shapes=[
+            pltpu.VMEM((padded * lats, lanes), jnp.float32),
             pltpu.SemaphoreType.DMA((devices,)),
             pltpu.SemaphoreType.DMA((devices,)),
         ],
-        compiler_params=pltpu.CompilerParams(collective_id=0, has_side_effects=True, vmem_limit_bytes=16 << 20),
+        compiler_params=pltpu.CompilerParams(collective_id=0, has_side_effects=True, vmem_limit_bytes=24 << 20),
         name="pair_tables",
-    )(table, mats)
+    )(table, mats, frames)
 
 
 def regrid_kernel(
-    strip_blocks, row_blocks, table_ref, frames_ref, mats_ref, out_ref,
-    wide, total, words_v, words_s, chosen, sem,
+    strip_blocks, row_blocks, table_ref, cells_ref, mats_ref, out_ref,
+    total, words_v, words_s, chosen, sem,
 ):
     devices, _, pairs = table_ref.shape
-    variables, lats, lanes = frames_ref.shape
-    padded = wide.shape[0] // lats
+    lats, padded, _ = cells_ref.shape
     blocks = out_ref.shape[0]
     me = lax.axis_index("space")
     source = table_ref[:, 0, :]
@@ -101,23 +124,14 @@
     words_v[...] = word + jnp.where(mine, MATCH, 0)
     move = pltpu.make_async_copy(words_v, words_s, sem)
     move.start()
-
-    wide[pl.ds(variables * lats, (padded - variables) * lats), :] = jnp.zeros(
-        ((padded - variables) * lats, lanes), jnp.float32
-    )
-
-    @pl.loop(0, variables)
-    def _(v):
-        wide[pl.ds(pl.multiple_of(v * lats, lats), lats), :] = frames_ref[v].astype(jnp.float32)
-
-    @pl.loop(0, blocks + 1)
-    def _(b):
-        total[b] = jnp.zeros(total.shape[1:], jnp.float32)
-
     move.wait()
 
     def scan_row(row, count):
         def scan(step, count):
+            clear = total.shape[0] // (devices * (pairs // 16))
+            first = (row * (pairs // 16) + step) * clear
+            for b in range(clear):
+                total[first + b] = jnp.zeros(total.shape[1:], jnp.float32)
             values = [words_s[row, step * 16 + lane] for lane in range(16)]
             places = [count]
             for value in values:
@@ -138,42 +152,40 @@
         for lane in range(GROUP):
             value = chosen[step * GROUP + lane] & (MATCH - 1)
             homes.append(value >> 11)
-            cells = wide[pl.ds((value >> 5) & 63, padded, stride=lats), :].astype(jnp.bfloat16)
             products.append(
                 lax.dot_general(
-                    mats_ref[value & 31], cells, (((1,), (1,)), ((), ())),
+                    mats_ref[value & 31], cells_ref[(value >> 5) & 63], (((1,), (1,)), ((), ())),
                     preferred_element_type=jnp.float32,
                 )
             )
         for home, product in zip(homes, products):
             total[home, :, :padded] += product
 
-    @pl.loop(0, blocks)
+    @pl.loop(0, blocks, unroll=4)
     def _(b):
         out_ref[b] = total[b].astype(jnp.bfloat16)
 
 
-def regrid(tables, frames, mats, blocks, strip_blocks, row_blocks):
+def regrid(tables, sources, mats, blocks, strip_blocks, row_blocks):
     devices, _, pairs = tables.shape
-    variables, lats, lanes = frames.shape
-    padded = -(-variables // 16) * 16
     cells = mats.shape[1]
+    steps = devices * (pairs // 16)
+    held = -(-(blocks + 1) // steps) * steps
     return pl.pallas_call(
         functools.partial(regrid_kernel, strip_blocks, row_blocks),
         out_shape=jax.ShapeDtypeStruct((blocks, cells, LANES), jnp.bfloat16),
         in_specs=[VMEM] * 3,
         out_specs=VMEM,
         scratch_shapes=[
-            pltpu.VMEM((padded * lats, lanes), jnp.float32),
-            pltpu.VMEM((blocks + 1, cells, LANES), jnp.float32),
+            pltpu.VMEM((held, cells, LANES), jnp.float32),
             pltpu.VMEM((devices, pairs), jnp.int32),
             pltpu.SMEM((devices, pairs), jnp.int32),
-            pltpu.SMEM((devices * pairs + 8,), jnp.int32),
+            pltpu.SMEM((devices * pairs + GROUP,), jnp.int32),
             pltpu.SemaphoreType.DMA,
         ],
         compiler_params=pltpu.CompilerParams(vmem_limit_bytes=40 << 20),
         name="regrid_pairs",
-    )(tables, frames, mats)
+    )(tables, sources, mats)
 
 
 def pack_fields(fields):
@@ -351,8 +363,8 @@
     strip_blocks = frames.shape[3] // SB
     row_blocks = strip_blocks * devices
     table = jnp.stack([pair_source, pair_matrix, pair_device[:, 0], pair_local])
-    tables, mats = gather_tables(table, regrid_mats, devices, strip_blocks)
-    part = regrid(tables, frames[0], mats, devices * BLK_DEV, strip_blocks, row_blocks)
+    tables, mats, sources = gather_tables(table, regrid_mats, frames[0], devices, strip_blocks)
+    part = regrid(tables, sources, mats, devices * BLK_DEV, strip_blocks, row_blocks)
     lift = LANES - w_first.shape[2]
     w1 = jnp.pad(w_first, ((0, 0), (0, 0), (0, lift), (0, 0))).reshape(3, 3 * LANES, -1)
     w2 = w_second.reshape(3, -1, w_second.shape[-1])

time: 48.9 us -> 43.9 us (0.90)
  Pallas kernels: 44.8 us -> 39.8 us
    pallas_call x1, Pallas kernels: 17.7 us -> 10.9 us  [regrid(): pl.pallas_call(functools.partial(regrid_kernel, strip_blocks, row_blocks)...]
    pallas_call x1, Pallas kernels: 6.25 us -> 9.21 us  [gather_tables(): pl.pallas_call(functools.partial(table_kernel, devices), out_shape=(jax.S...]
    pallas_call x1, Pallas kernels: 20.8 us -> 19.7 us  [encode(): pl.pallas_call(functools.partial(encode_kernel, chips), out_shape=jax.Sha...]
where the time goes in v3:
time: 43.9 us; the launch traced here: 43.8 us
  Pallas kernels  39.8 us (91%)
  local copies, waits for them, and re-layouts  3.13 us (7%)
  other arithmetic  0.71 us (2%)
    pallas_call x1, Pallas kernels, encode(): pl.pallas_call(functools.partial(encode_kernel, chips), out_shape=jax.Sha...  19.7 us
    pallas_call x1, Pallas kernels, regrid(): pl.pallas_call(functools.partial(regrid_kernel, strip_blocks, row_blocks)...  10.9 us
    pallas_call x1, Pallas kernels, gather_tables(): pl.pallas_call(functools.partial(table_kernel, devices), out_shape=(jax.S...  9.21 us
    unnamed x13, local copies, waits for them, and re-layouts  3.09 us

profile of v3, /device:TPU:0, one launch (start us, length us, event | category | flops | bytes accessed | tf_op | source)
XLA Modules:
  0.0 43.8 jit_solution(1124776229157334723)
XLA Ops:
  0.0 0.7 %pad_add_fusion.table_ref = s32[4,128]{1,0:T(4,128)S(1)} fusion(s32[1,128]{1,0:T(1,128)} %bitcast.16, s32[1,128]{1,0:T(1,128)} %bitcast.17, s32[1,128]{1,0:T(1,128)} %bitcast.18, s32[1,128]{1,0:T(1,128)} %bitcast.19), kind=kLoop, calls=%fused_computation | loop fusion | flops 1536 | bytes 4096 | tf_op jit(solution)/shard_map/stack | solution.py:365
  0.7 0.0 copy-start
  0.7 1.3 %copy-done = bf16[1,73,64,128]{3,2,1,0:T(8,128)(2,1)S(1)} copy-done((bf16[1,73,64,128]{3,2,1,0:T(8,128)(2,1)S(1)}, bf16[1,73,64,128]{3,2,1,0:T(8,128)(2,1)}, u32[]{:S(2)}) %copy-start) | copy-done | bytes 1196056
  2.0 0.0 copy-start.2
  2.0 1.0 %copy-done.2 = bf16[16,64,144]{2,1,0:T(8,128)(2,1)S(1)} copy-done((bf16[16,64,144]{2,1,0:T(8,128)(2,1)S(1)}, bf16[16,64,144]{2,1,0:T(8,128)(2,1)}, u32[]{:S(2)}) %copy-start.2) | copy-done | bytes 294936
  3.0 9.2 %pair_tables.1 = (s32[8,4,128]{2,1,0:T(4,128)S(1)}, bf16[32,144,128]{2,1,0:T(8,128)(2,1)S(1)}, bf16[64,80,128]{2,1,0:T(8,128)(2,1)S(1)}) custom-call(s32[4,128]{1,0:T(4,128)S(1)} %pad_add_fusion.table_ref, bf16[16,64,144]{2,1,0:T(8,128)(2,1)S(1)} %copy-done.2, bf16[73,64,128]{2,1,0:T(8,128)(2,1)S(1)} %bitcast.12), custom_call_target="tpu_custom_call" | custom-call | tf_op jit(solution)/shard_map/pair_tables/pallas_call | solution.py:89
  12.3 0.0 copy-start.5
  12.3 0.0 copy-start.1
  12.3 0.0 copy-start.3
  12.3 0.0 copy-start.4
  12.3 10.9 %regrid_pairs.1.part_ref = bf16[96,144,128]{2,1,0:T(8,128)(2,1)S(1)} custom-call(s32[8,4,128]{2,1,0:T(4,128)S(1)} %get-tuple-element.8.table_ref, bf16[64,80,128]{2,1,0:T(8,128)(2,1)S(1)} %get-tuple-element.9.cells_ref, bf16[32,144,128]{2,1,0:T(8,128)(2,1)S(1)} %get-tuple-element.10.mats_ref), custom_call_target="tpu_custom_call" | custom-call | tf_op jit(solution)/shard_map/regrid_pairs/pallas_call | solution.py:174
  23.2 0.0 copy-done.5
  23.3 0.0 copy-done.1
  23.3 0.0 copy-done.3
  23.3 0.0 copy-done.4
  23.3 19.7 %reduce_and_encode.1 = bf16[12,64,256]{2,1,0:T(8,128)(2,1)S(1)} custom-call(bf16[96,144,128]{2,1,0:T(8,128)(2,1)S(1)} %regrid_pairs.1.part_ref, bf16[3,384,256]{2,1,0:T(8,128)(2,1)S(1)} %bitcast.10, f32[1,256]{1,0:T(1,128)S(1)} %bitcast.14, bf16[3,768,256]{2,1,0:T(8,128)(2,1)S(1)} %bitcast.13, f32[1,256]{1,0:T(1,128)S(1)} %bitcast.15), custom_call_target="tpu_custom_call" | custom-call | tf_op jit(solution)/shard_map/reduce_and_encode/pallas_call | solution.py:328
  43.0 0.7 %copy.12 = bf16[1,12,64,256]{3,2,1,0:T(8,128)(2,1)} copy(bf16[1,12,64,256]{3,2,1,0:T(8,128)(2,1)S(1)} %bitcast.11) | data formatting | bytes 786432
  (1 shorter events, 0.0 us)
Async XLA Ops:
  0.7 1.3 %copy-start = (bf16[1,73,64,128]{3,2,1,0:T(8,128)(2,1)S(1)}, bf16[1,73,64,128]{3,2,1,0:T(8,128)(2,1)}, u32[]{:S(2)}) copy-start(bf16[1,73,64,128]{3,2,1,0:T(8,128)(2,1)} %param.10) | copy-start | bytes 3588100
  2.0 1.0 %copy-start.2 = (bf16[16,64,144]{2,1,0:T(8,128)(2,1)S(1)}, bf16[16,64,144]{2,1,0:T(8,128)(2,1)}, u32[]{:S(2)}) copy-start(bf16[16,64,144]{2,1,0:T(8,128)(2,1)} %mats_ref.1) | copy-start | bytes 884740
  12.3 11.0 %copy-start.5 = (bf16[3,3,73,256]{3,2,1,0:T(8,128)(2,1)S(1)}, bf16[3,3,73,256]{3,2,1,0:T(8,128)(2,1)}, u32[]{:S(2)}) copy-start(bf16[3,3,73,256]{3,2,1,0:T(8,128)(2,1)} %param.16) | copy-start | bytes 1009156
  12.3 11.0 %copy-start.1 = (bf16[3,3,256,256]{3,2,1,0:T(8,128)(2,1)S(1)}, bf16[3,3,256,256]{3,2,1,0:T(8,128)(2,1)}, u32[]{:S(2)}) copy-start(bf16[3,3,256,256]{3,2,1,0:T(8,128)(2,1)} %param.18) | copy-start | bytes 3538948
  12.3 11.0 %copy-start.3 = (f32[256]{0:T(256)S(1)}, f32[256]{0:T(256)}, u32[]{:S(2)}) copy-start(f32[256]{0:T(256)} %param.17) | copy-start | bytes 3076
  12.3 11.0 %copy-start.4 = (f32[256]{0:T(256)S(1)}, f32[256]{0:T(256)}, u32[]{:S(2)}) copy-start(f32[256]{0:T(256)} %param.19) | copy-start | bytes 3076

commit v4 on v3

--- a/solution.py
+++ b/solution.py
@@ -14,6 +14,7 @@
 
 MESH = pl.DeviceIdType.MESH
 VMEM = pl.BlockSpec(memory_space=pltpu.VMEM)
+HBM = pl.BlockSpec(memory_space=pltpu.HBM)
 LANES = 128
 ROW = 16
 GROUP = 8
@@ -31,9 +32,16 @@
 
 
 def table_kernel(
-    devices, table_ref, mats_ref, frames_ref, all_ref, turned_ref, cells_ref, wide, send_sem, recv_sem
+    devices, table_ref, mats_hbm, frames_hbm, all_ref, turned_ref, cells_ref,
+    mats_ref, frames_ref, wide, load_sem, send_sem, recv_sem,
 ):
     me = lax.axis_index("space")
+    loads = [
+        pltpu.make_async_copy(mats_hbm, mats_ref, load_sem.at[0]),
+        pltpu.make_async_copy(frames_hbm, frames_ref, load_sem.at[1]),
+    ]
+    for load in loads:
+        load.start()
     barrier = pltpu.get_barrier_semaphore()
     for step in range(1, devices):
         peer = lax.rem(me + step, devices)
@@ -43,6 +51,20 @@
     wide[pl.ds(variables * lats, (padded - variables) * lats), :] = jnp.zeros(
         ((padded - variables) * lats, lanes), jnp.float32
     )
+    loads[0].wait()
+    strip_blocks = turned_ref.shape[0] // mats_ref.shape[0]
+
+    @pl.loop(0, mats_ref.shape[0])
+    def _(m):
+        matrix = mats_ref[m].astype(jnp.float32)
+        blank = jnp.zeros_like(matrix)
+        for place in range(strip_blocks):
+            stack = [matrix if other == place else blank for other in range(strip_blocks)]
+            turned_ref[m * strip_blocks + place] = (
+                jnp.concatenate(stack, axis=0).T.astype(jnp.bfloat16)
+            )
+
+    loads[1].wait()
 
     @pl.loop(0, variables)
     def _(v):
@@ -62,19 +84,8 @@
         copy.start()
         copies.append(copy)
     all_ref[me] = table_ref[...]
-    strip_blocks = turned_ref.shape[0] // mats_ref.shape[0]
-
-    @pl.loop(0, mats_ref.shape[0])
-    def _(m):
-        matrix = mats_ref[m].astype(jnp.float32)
-        blank = jnp.zeros_like(matrix)
-        for place in range(strip_blocks):
-            stack = [matrix if other == place else blank for other in range(strip_blocks)]
-            turned_ref[m * strip_blocks + place] = (
-                jnp.concatenate(stack, axis=0).T.astype(jnp.bfloat16)
-            )
-
-    @pl.loop(0, lats)
+
+    @pl.loop(0, lats, unroll=4)
     def _(lat):
         cells_ref[lat] = wide[pl.ds(lat, padded, stride=lats), :].astype(jnp.bfloat16)
 
@@ -93,10 +104,13 @@
             jax.ShapeDtypeStruct(turned, mats.dtype),
             jax.ShapeDtypeStruct((lats, padded, lanes), frames.dtype),
         ),
-        in_specs=[VMEM] * 3,
+        in_specs=[VMEM, HBM, HBM],
         out_specs=(VMEM, VMEM, VMEM),
         scratch_shapes=[
+            pltpu.VMEM(mats.shape, mats.dtype),
+            pltpu.VMEM(frames.shape, frames.dtype),
             pltpu.VMEM((padded * lats, lanes), jnp.float32),
+            pltpu.SemaphoreType.DMA((2,)),
             pltpu.SemaphoreType.DMA((devices,)),
             pltpu.SemaphoreType.DMA((devices,)),
         ],

time: 43.9 us -> 43.3 us (0.986); the launches traced: 43.8 us -> 42.7 us
  Pallas kernels: 39.8 us -> 38.7 us
    pallas_call x1, Pallas kernels: 19.7 us -> 18.5 us  [encode(): pl.pallas_call(functools.partial(encode_kernel, chips), out_shape=jax.Sha...]
    pallas_call x1, Pallas kernels: 10.9 us -> 11.5 us  [regrid(): pl.pallas_call(functools.partial(regrid_kernel, strip_blocks, row_blocks)...]
    pallas_call x1, Pallas kernels: 9.21 us -> 8.64 us  [gather_tables(): pl.pallas_call(functools.partial(table_kernel, devices), out_shape=(jax.S...]
where the time goes in v4:
time: 43.3 us; the launch traced here: 42.7 us
  Pallas kernels  38.7 us (89%)
  local copies, waits for them, and re-layouts  3.13 us (7%)
  other arithmetic  0.71 us (2%)
    pallas_call x1, Pallas kernels, encode(): pl.pallas_call(functools.partial(encode_kernel, chips), out_shape=jax.Sha...  18.5 us
    pallas_call x1, Pallas kernels, regrid(): pl.pallas_call(functools.partial(regrid_kernel, strip_blocks, row_blocks)...  11.5 us
    pallas_call x1, Pallas kernels, gather_tables(): pl.pallas_call(functools.partial(table_kernel, devices), out_shape=(jax.S...  8.64 us
    unnamed x13, local copies, waits for them, and re-layouts  3.09 us

profile of v4, /device:TPU:0, one launch (start us, length us, event | category | flops | bytes accessed | tf_op | source)
XLA Modules:
  0.0 42.7 jit_solution(85728812440372779)
XLA Ops:
  0.0 0.7 %pad_add_fusion.table_ref = s32[4,128]{1,0:T(4,128)S(1)} fusion(s32[1,128]{1,0:T(1,128)} %bitcast.16, s32[1,128]{1,0:T(1,128)} %bitcast.17, s32[1,128]{1,0:T(1,128)} %bitcast.18, s32[1,128]{1,0:T(1,128)} %bitcast.19), kind=kLoop, calls=%fused_computation | loop fusion | flops 1536 | bytes 4096 | tf_op jit(solution)/shard_map/stack | solution.py:379
  0.7 0.0 copy-start
  0.7 1.3 %copy-done = bf16[1,73,64,128]{3,2,1,0:T(8,128)(2,1)S(1)} copy-done((bf16[1,73,64,128]{3,2,1,0:T(8,128)(2,1)S(1)}, bf16[1,73,64,128]{3,2,1,0:T(8,128)(2,1)}, u32[]{:S(2)}) %copy-start) | copy-done | bytes 1196056
  2.0 0.0 copy-start.2
  2.0 1.0 %copy-done.2 = bf16[16,64,144]{2,1,0:T(8,128)(2,1)S(1)} copy-done((bf16[16,64,144]{2,1,0:T(8,128)(2,1)S(1)}, bf16[16,64,144]{2,1,0:T(8,128)(2,1)}, u32[]{:S(2)}) %copy-start.2) | copy-done | bytes 294936
  3.0 8.6 %pair_tables.1 = (s32[8,4,128]{2,1,0:T(4,128)S(1)}, bf16[32,144,128]{2,1,0:T(8,128)(2,1)S(1)}, bf16[64,80,128]{2,1,0:T(8,128)(2,1)S(1)}) custom-call(s32[4,128]{1,0:T(4,128)S(1)} %pad_add_fusion.table_ref, bf16[16,64,144]{2,1,0:T(8,128)(2,1)S(1)} %copy-done.2, bf16[73,64,128]{2,1,0:T(8,128)(2,1)S(1)} %bitcast.12), custom_call_target="tpu_custom_call" | custom-call | tf_op jit(solution)/shard_map/pair_tables/pallas_call | solution.py:100
  11.7 0.0 copy-start.5
  11.7 0.0 copy-start.1
  11.7 0.0 copy-start.3
  11.7 0.0 copy-start.4
  11.7 11.5 %regrid_pairs.1.part_ref = bf16[96,144,128]{2,1,0:T(8,128)(2,1)S(1)} custom-call(s32[8,4,128]{2,1,0:T(4,128)S(1)} %get-tuple-element.8.table_ref, bf16[64,80,128]{2,1,0:T(8,128)(2,1)S(1)} %get-tuple-element.9.cells_ref, bf16[32,144,128]{2,1,0:T(8,128)(2,1)S(1)} %get-tuple-element.10.mats_ref), custom_call_target="tpu_custom_call" | custom-call | tf_op jit(solution)/shard_map/regrid_pairs/pallas_call | solution.py:188
  23.3 0.0 copy-done.5
  23.3 0.0 copy-done.1
  23.3 0.0 copy-done.3
  23.4 0.0 copy-done.4
  23.4 18.5 %reduce_and_encode.1 = bf16[12,64,256]{2,1,0:T(8,128)(2,1)S(1)} custom-call(bf16[96,144,128]{2,1,0:T(8,128)(2,1)S(1)} %regrid_pairs.1.part_ref, bf16[3,384,256]{2,1,0:T(8,128)(2,1)S(1)} %bitcast.10, f32[1,256]{1,0:T(1,128)S(1)} %bitcast.14, bf16[3,768,256]{2,1,0:T(8,128)(2,1)S(1)} %bitcast.13, f32[1,256]{1,0:T(1,128)S(1)} %bitcast.15), custom_call_target="tpu_custom_call" | custom-call | tf_op jit(solution)/shard_map/reduce_and_encode/pallas_call | solution.py:342
  41.9 0.7 %copy.12 = bf16[1,12,64,256]{3,2,1,0:T(8,128)(2,1)} copy(bf16[1,12,64,256]{3,2,1,0:T(8,128)(2,1)S(1)} %bitcast.11) | data formatting | bytes 786432
  (1 shorter events, 0.0 us)
Async XLA Ops:
  0.7 1.3 %copy-start = (bf16[1,73,64,128]{3,2,1,0:T(8,128)(2,1)S(1)}, bf16[1,73,64,128]{3,2,1,0:T(8,128)(2,1)}, u32[]{:S(2)}) copy-start(bf16[1,73,64,128]{3,2,1,0:T(8,128)(2,1)} %param.10) | copy-start | bytes 3588100
  2.0 1.0 %copy-start.2 = (bf16[16,64,144]{2,1,0:T(8,128)(2,1)S(1)}, bf16[16,64,144]{2,1,0:T(8,128)(2,1)}, u32[]{:S(2)}) copy-start(bf16[16,64,144]{2,1,0:T(8,128)(2,1)} %mats_hbm.1) | copy-start | bytes 884740
  11.7 11.6 %copy-start.5 = (bf16[3,3,73,256]{3,2,1,0:T(8,128)(2,1)S(1)}, bf16[3,3,73,256]{3,2,1,0:T(8,128)(2,1)}, u32[]{:S(2)}) copy-start(bf16[3,3,73,256]{3,2,1,0:T(8,128)(2,1)} %param.16) | copy-start | bytes 1009156
  11.7 11.6 %copy-start.1 = (bf16[3,3,256,256]{3,2,1,0:T(8,128)(2,1)S(1)}, bf16[3,3,256,256]{3,2,1,0:T(8,128)(2,1)}, u32[]{:S(2)}) copy-start(bf16[3,3,256,256]{3,2,1,0:T(8,128)(2,1)} %param.18) | copy-start | bytes 3538948
  11.7 11.6 %copy-start.3 = (f32[256]{0:T(256)S(1)}, f32[256]{0:T(256)}, u32[]{:S(2)}) copy-start(f32[256]{0:T(256)} %param.17) | copy-start | bytes 3076
  11.7 11.6 %copy-start.4 = (f32[256]{0:T(256)S(1)}, f32[256]{0:T(256)}, u32[]{:S(2)}) copy-start(f32[256]{0:T(256)} %param.19) | copy-start | bytes 3076

commit v5 on v4

--- a/solution.py
+++ b/solution.py
@@ -17,7 +17,7 @@
 HBM = pl.BlockSpec(memory_space=pltpu.HBM)
 LANES = 128
 ROW = 16
-GROUP = 8
+GROUP = 16
 CHUNKS = 3
 MATCH = 1 << 20
 FRONT = 64

time: 43.3 us -> 42.3 us (0.977)
  Pallas kernels: 38.7 us -> 38.1 us
    pallas_call x1, Pallas kernels: 11.5 us -> 9.33 us  [regrid(): pl.pallas_call(functools.partial(regrid_kernel, strip_blocks, row_blocks)...]
    pallas_call x1, Pallas kernels: 18.5 us -> 20.1 us  [encode(): pl.pallas_call(functools.partial(encode_kernel, chips), out_shape=jax.Sha...]
where the time goes in v5:
time: 42.3 us; the launch traced here: 42.1 us
  Pallas kernels  38.1 us (90%)
  local copies, waits for them, and re-layouts  3.13 us (7%)
  other arithmetic  0.71 us (2%)
    pallas_call x1, Pallas kernels, encode(): pl.pallas_call(functools.partial(encode_kernel, chips), out_shape=jax.Sha...  20.1 us
    pallas_call x1, Pallas kernels, regrid(): pl.pallas_call(functools.partial(regrid_kernel, strip_blocks, row_blocks)...  9.33 us
    pallas_call x1, Pallas kernels, gather_tables(): pl.pallas_call(functools.partial(table_kernel, devices), out_shape=(jax.S...  8.64 us
    unnamed x13, local copies, waits for them, and re-layouts  3.09 us

profile of v5, /device:TPU:0, one launch (start us, length us, event | category | flops | bytes accessed | tf_op | source)
XLA Modules:
  0.0 42.1 jit_solution(1499361647701579460)
XLA Ops:
  0.0 0.7 %pad_add_fusion.table_ref = s32[4,128]{1,0:T(4,128)S(1)} fusion(s32[1,128]{1,0:T(1,128)} %bitcast.16, s32[1,128]{1,0:T(1,128)} %bitcast.17, s32[1,128]{1,0:T(1,128)} %bitcast.18, s32[1,128]{1,0:T(1,128)} %bitcast.19), kind=kLoop, calls=%fused_computation | loop fusion | flops 1536 | bytes 4096 | tf_op jit(solution)/shard_map/stack | solution.py:379
  0.7 0.0 copy-start
  0.7 1.3 %copy-done = bf16[1,73,64,128]{3,2,1,0:T(8,128)(2,1)S(1)} copy-done((bf16[1,73,64,128]{3,2,1,0:T(8,128)(2,1)S(1)}, bf16[1,73,64,128]{3,2,1,0:T(8,128)(2,1)}, u32[]{:S(2)}) %copy-start) | copy-done | bytes 1196056
  2.0 0.0 copy-start.2
  2.0 1.0 %copy-done.2 = bf16[16,64,144]{2,1,0:T(8,128)(2,1)S(1)} copy-done((bf16[16,64,144]{2,1,0:T(8,128)(2,1)S(1)}, bf16[16,64,144]{2,1,0:T(8,128)(2,1)}, u32[]{:S(2)}) %copy-start.2) | copy-done | bytes 294936
  3.0 8.6 %pair_tables.1 = (s32[8,4,128]{2,1,0:T(4,128)S(1)}, bf16[32,144,128]{2,1,0:T(8,128)(2,1)S(1)}, bf16[64,80,128]{2,1,0:T(8,128)(2,1)S(1)}) custom-call(s32[4,128]{1,0:T(4,128)S(1)} %pad_add_fusion.table_ref, bf16[16,64,144]{2,1,0:T(8,128)(2,1)S(1)} %copy-done.2, bf16[73,64,128]{2,1,0:T(8,128)(2,1)S(1)} %bitcast.12), custom_call_target="tpu_custom_call" | custom-call | tf_op jit(solution)/shard_map/pair_tables/pallas_call | solution.py:100
  11.7 0.0 copy-start.5
  11.7 0.0 copy-start.1
  11.7 0.0 copy-start.3
  11.7 0.0 copy-start.4
  11.7 9.3 %regrid_pairs.1.part_ref = bf16[96,144,128]{2,1,0:T(8,128)(2,1)S(1)} custom-call(s32[8,4,128]{2,1,0:T(4,128)S(1)} %get-tuple-element.8.table_ref, bf16[64,80,128]{2,1,0:T(8,128)(2,1)S(1)} %get-tuple-element.9.cells_ref, bf16[32,144,128]{2,1,0:T(8,128)(2,1)S(1)} %get-tuple-element.10.mats_ref), custom_call_target="tpu_custom_call" | custom-call | tf_op jit(solution)/shard_map/regrid_pairs/pallas_call | solution.py:188
  21.1 0.0 copy-done.5
  21.1 0.0 copy-done.1
  21.1 0.0 copy-done.3
  21.1 0.0 copy-done.4
  21.2 20.1 %reduce_and_encode.1 = bf16[12,64,256]{2,1,0:T(8,128)(2,1)S(1)} custom-call(bf16[96,144,128]{2,1,0:T(8,128)(2,1)S(1)} %regrid_pairs.1.part_ref, bf16[3,384,256]{2,1,0:T(8,128)(2,1)S(1)} %bitcast.10, f32[1,256]{1,0:T(1,128)S(1)} %bitcast.14, bf16[3,768,256]{2,1,0:T(8,128)(2,1)S(1)} %bitcast.13, f32[1,256]{1,0:T(1,128)S(1)} %bitcast.15), custom_call_target="tpu_custom_call" | custom-call | tf_op jit(solution)/shard_map/reduce_and_encode/pallas_call | solution.py:342
  41.3 0.7 %copy.12 = bf16[1,12,64,256]{3,2,1,0:T(8,128)(2,1)} copy(bf16[1,12,64,256]{3,2,1,0:T(8,128)(2,1)S(1)} %bitcast.11) | data formatting | bytes 786432
  (1 shorter events, 0.0 us)
Async XLA Ops:
  0.7 1.3 %copy-start = (bf16[1,73,64,128]{3,2,1,0:T(8,128)(2,1)S(1)}, bf16[1,73,64,128]{3,2,1,0:T(8,128)(2,1)}, u32[]{:S(2)}) copy-start(bf16[1,73,64,128]{3,2,1,0:T(8,128)(2,1)} %param.10) | copy-start | bytes 3588100
  2.0 1.0 %copy-start.2 = (bf16[16,64,144]{2,1,0:T(8,128)(2,1)S(1)}, bf16[16,64,144]{2,1,0:T(8,128)(2,1)}, u32[]{:S(2)}) copy-start(bf16[16,64,144]{2,1,0:T(8,128)(2,1)} %mats_hbm.1) | copy-start | bytes 884740
  11.7 9.4 %copy-start.5 = (bf16[3,3,73,256]{3,2,1,0:T(8,128)(2,1)S(1)}, bf16[3,3,73,256]{3,2,1,0:T(8,128)(2,1)}, u32[]{:S(2)}) copy-start(bf16[3,3,73,256]{3,2,1,0:T(8,128)(2,1)} %param.16) | copy-start | bytes 1009156
  11.7 9.4 %copy-start.1 = (bf16[3,3,256,256]{3,2,1,0:T(8,128)(2,1)S(1)}, bf16[3,3,256,256]{3,2,1,0:T(8,128)(2,1)}, u32[]{:S(2)}) copy-start(bf16[3,3,256,256]{3,2,1,0:T(8,128)(2,1)} %param.18) | copy-start | bytes 3538948
  11.7 9.4 %copy-start.3 = (f32[256]{0:T(256)S(1)}, f32[256]{0:T(256)}, u32[]{:S(2)}) copy-start(f32[256]{0:T(256)} %param.17) | copy-start | bytes 3076
  11.7 9.4 %copy-start.4 = (f32[256]{0:T(256)S(1)}, f32[256]{0:T(256)}, u32[]{:S(2)}) copy-start(f32[256]{0:T(256)} %param.19) | copy-start | bytes 3076
